TPU v7x, 1024 devices: a whole 4x8x16 slice. The times are simulated.
1024 devices in a mesh: dp: 16 (over z), ctx: 8 (over x, core), tp: 8 (over y).
Axes of the slice: x: 4, y: 8, z: 16, core: 2. Of those that a mesh axis runs over, the one named last changes fastest.
Arguments:
- tokens: bfloat16 [4096, 4096], P(('dp', 'ctx', 'tp')), may hold values from -24 to 24
- out_grad: bfloat16 [4096, 4096], P(('dp', 'ctx', 'tp')), may hold values from -6 to 6
- expert_ids: int32 [4096, 2], P(('dp', 'ctx', 'tp')), may hold values from 0 to 7, all different within a row; in each aligned block of 4 rows (0 to 3, 4 to 7, ...) at most 2 rows name the same one
- gates: bfloat16 [4096, 2], P(('dp', 'ctx', 'tp')), may hold values from 0.25 to 1
- gate_proj: bfloat16 [8, 1536, 4096], P('ctx', 'tp'), may hold values from -0.09375 to 0.09375
- up_proj: bfloat16 [8, 1536, 4096], P('ctx', 'tp'), may hold values from -0.09375 to 0.09375
- down_proj: bfloat16 [8, 1536, 4096], P('ctx', 'tp'), may hold values from -0.15625 to 0.15625
Outputs:
- token_grad: bfloat16 [4096, 4096], P(('dp', 'ctx', 'tp'))
- gate_proj_grad: float32 [8, 1536, 4096], P('ctx', 'tp', 'dp')
- up_proj_grad: float32 [8, 1536, 4096], P('ctx', 'tp', 'dp')
- down_proj_grad: float32 [8, 1536, 4096], P('ctx', 'tp', 'dp')
Inputs may be any that keep to these rules, and one draw needn't show every extreme that they name: `expert_ids`: each token names 2 different experts. Among the 4 tokens of one device (aligned blocks of rows) no expert is named more than 2 times, and that bound is reached in every draw.
All inputs are finite; a program needn't handle non-finite values.
Results may differ from a plain program's by a relative error of at most 0.02.
Values may be sent and summed in bfloat16 or wider, within the bound.
A program may use at most 32 MiB of HBM per device.

v0:
```python
import math

import jax
import jax.numpy as jnp
from jax import lax
from jax.sharding import PartitionSpec as P


def silu_parts(pre_gate):
    sigmoid_part = jax.nn.sigmoid(pre_gate)
    return (pre_gate * sigmoid_part, sigmoid_part * (1.0 + pre_gate * (1.0 - sigmoid_part)))


def local(tokens, out_grad, expert_ids, gates, gate_proj, up_proj, down_proj):
    n_ctx = lax.axis_size("ctx")
    n_tp = lax.axis_size("tp")
    n_dp = lax.axis_size("dp")
    tok_count, model_width = tokens.shape
    top_count = expert_ids.shape[1]
    experts = gate_proj.shape[0] * n_ctx
    capacity = max(2, 2 * tok_count * top_count // experts)
    tokens_all = tok_count * n_dp * n_ctx * n_tp
    grad_scale = 1.0 / math.sqrt(tokens_all)
    choice_ids = expert_ids.reshape(-1)
    onehot = (choice_ids[:, None] == jnp.arange(experts, dtype=jnp.int32)[None, :]).astype(
        jnp.int32
    )
    before = jnp.cumsum(onehot, axis=0) - onehot
    slot_index = jnp.sum(before * onehot, axis=1)
    position = choice_ids * capacity + slot_index
    placing = jnp.arange(experts * capacity, dtype=jnp.int32)[:, None] == position[None, :]
    placing_tokens = jnp.sum(
        placing.reshape(experts * capacity, tok_count, top_count), axis=2
    ).astype(jnp.bfloat16)
    gate_flat = gates.reshape(-1).astype(jnp.float32)
    placing_gates = jnp.sum(
        jnp.where(placing, gate_flat[None, :], 0.0).reshape(
            experts * capacity, tok_count, top_count
        ),
        axis=2,
    )
    send_rows = jnp.dot(placing_tokens, tokens, preferred_element_type=jnp.float32).astype(
        jnp.bfloat16
    )
    send_grads = jnp.dot(
        placing_gates, out_grad.astype(jnp.float32), preferred_element_type=jnp.float32
    ).astype(jnp.bfloat16)
    send_rows = send_rows.reshape(experts, capacity, model_width)
    send_grads = send_grads.reshape(experts, capacity, model_width)
    got_rows, got_grads = (
        lax.all_to_all(send_rows, "ctx", split_axis=0, concat_axis=0, tiled=True),
        lax.all_to_all(send_grads, "ctx", split_axis=0, concat_axis=0, tiled=True),
    )
    recv_rows, recv_grads = (
        lax.all_gather(got_rows[:, None], "tp", axis=1, tiled=True),
        lax.all_gather(got_grads[:, None], "tp", axis=1, tiled=True),
    )
    rows_x = recv_rows.reshape(-1, model_width)
    rows_dy = recv_grads.reshape(-1, model_width)
    gate_w = gate_proj[0]
    up_w = up_proj[0]
    down_w = down_proj[0]
    contract_last = (((1,), (1,)), ((), ()))
    pre_gate = lax.dot_general(rows_x, gate_w, contract_last, preferred_element_type=jnp.float32)
    pre_up = lax.dot_general(rows_x, up_w, contract_last, preferred_element_type=jnp.float32)
    activated, slope = silu_parts(pre_gate)
    hidden = (activated * pre_up).astype(jnp.bfloat16)
    d_hidden = lax.dot_general(rows_dy, down_w, contract_last, preferred_element_type=jnp.float32)
    d_up = (d_hidden * activated).astype(jnp.bfloat16)
    d_gate = (d_hidden * pre_up * slope).astype(jnp.bfloat16)
    partial_grad = jnp.dot(d_gate, gate_w, preferred_element_type=jnp.float32) + jnp.dot(
        d_up, up_w, preferred_element_type=jnp.float32
    )
    shares = lax.psum_scatter(
        partial_grad.reshape(n_ctx, n_tp, capacity, model_width).astype(jnp.bfloat16),
        "tp",
        scatter_dimension=1,
        tiled=True,
    )
    expert_grad = lax.all_to_all(shares, "ctx", split_axis=0, concat_axis=0, tiled=True)
    expert_grad = expert_grad.reshape(experts * capacity, model_width)
    picked = lax.dot_general(
        placing.astype(jnp.bfloat16),
        expert_grad,
        (((0,), (0,)), ((), ())),
        preferred_element_type=jnp.float32,
    )
    token_grad = jnp.sum(picked.reshape(tok_count, top_count, model_width), axis=1).astype(
        jnp.bfloat16
    )
    contract_first = (((0,), (0,)), ((), ()))
    gate_term = lax.dot_general(d_gate, rows_x, contract_first, preferred_element_type=jnp.float32)
    up_term = lax.dot_general(d_up, rows_x, contract_first, preferred_element_type=jnp.float32)
    down_term = lax.dot_general(hidden, rows_dy, contract_first, preferred_element_type=jnp.float32)
    gate_sum, up_sum, down_sum = (
        lax.psum_scatter(
            gate_term.astype(jnp.bfloat16), "dp", scatter_dimension=1, tiled=True
        ).astype(jnp.float32),
        lax.psum_scatter(
            up_term.astype(jnp.bfloat16), "dp", scatter_dimension=1, tiled=True
        ).astype(jnp.float32),
        lax.psum_scatter(
            down_term.astype(jnp.bfloat16), "dp", scatter_dimension=1, tiled=True
        ).astype(jnp.float32),
    )
    return (
        token_grad,
        (gate_sum * grad_scale)[None],
        (up_sum * grad_scale)[None],
        (down_sum * grad_scale)[None],
    )


def solution(mesh):
    placed = (
        P(("dp", "ctx", "tp"), None),
        P(("dp", "ctx", "tp"), None),
        P(("dp", "ctx", "tp"), None),
        P(("dp", "ctx", "tp"), None),
        P("ctx", "tp", None),
        P("ctx", "tp", None),
        P("ctx", "tp", None),
    )
    return jax.shard_map(
        local,
        mesh=mesh,
        in_specs=placed,
        out_specs=(
            P(("dp", "ctx", "tp"), None),
            P("ctx", "tp", "dp"),
            P("ctx", "tp", "dp"),
            P("ctx", "tp", "dp"),
        ),
        check_vma=False,
    )
```

profile of v0, /device:TPU:4, one launch (start us, length us, event | category | flops | bytes accessed | tf_op | source)
XLA Modules:
  0.0 417.4 jit_solution(3428269037695649197)
XLA Ops:
  8.7 1.0 convolution_convert_fusion.3
  9.8 19.0 %all_to_all.15 = bf16[8,2,4096]{2,1,0:T(2,128)(2,1)S(1)} all-to-all(bf16[8,2,4096]{2,1,0:T(2,128)(2,1)S(1)} %reshape.95), channel_id=1, replica_groups=mesh['dp'=16,'ctx'=8,'tp'=8] {'ctx'}, dimensions={0} | all-to-all | bytes 262144 | tf_op jit(solution)/shard_map/all_to_all | solution.py:51
  30.4 1.0 fusion.16
  31.5 8.5 %all_to_all.16 = bf16[8,2,4096]{2,1,0:T(2,128)(2,1)S(1)} all-to-all(bf16[8,2,4096]{2,1,0:T(2,128)(2,1)S(1)} %reshape.93), channel_id=1, replica_groups=mesh['dp'=16,'ctx'=8,'tp'=8] {'ctx'}, dimensions={0} | all-to-all | bytes 262144 | tf_op jit(solution)/shard_map/all_to_all | solution.py:52
  40.8 32.3 %all-gather.7.cloned.1.call-done = bf16[8,16,4096]{2,0,1:T(8,128)(2,1)} async-done(((bf16[8,2,4096]{2,0,1:T(8,128)(2,1)}), bf16[8,16,4096]{2,0,1:T(8,128)(2,1)}) %all-gather.7.cloned.1.call-update) | async-done | bytes 1048592 | tf_op jit(solution)/shard_map/all_gather | solution.py:55
  73.1 1.8 copy.53
  76.9 44.8 %all-gather.5.cloned.1.call-done = bf16[8,16,4096]{2,0,1:T(8,128)(2,1)} async-done(((bf16[8,2,4096]{2,0,1:T(8,128)(2,1)}), bf16[8,16,4096]{2,0,1:T(8,128)(2,1)}) %all-gather.5.cloned.1.call-update) | async-done | bytes 1048592 | tf_op jit(solution)/shard_map/all_gather | solution.py:56
  121.7 1.9 copy.51
  125.6 1.5 fusion
  127.1 2.5 convert_element_type.69
  129.6 2.8 copy.54
  132.5 2.9 convolution_convert_fusion
  135.6 1.7 convolution_convert_fusion.1
  137.3 1.7 convolution_convert_fusion.2
  139.1 39.0 %reduce-scatter.5.cloned.1.call-done = bf16[8,1,2,4096]{3,0,2,1:T(8,128)(2,1)} async-done(((bf16[8,8,2,4096]{3,0,2,1:T(8,128)(2,1)}), bf16[8,1,2,4096]{3,0,2,1:T(8,128)(2,1)}) %reduce-scatter.5.cloned.1.call-update) | async-done | bytes 131088 | tf_op jit(solution)/shard_map/reduce_scatter | solution.py:74
  178.1 1.7 copy.55
  179.7 4.8 %all-to-all-start.2 = ((bf16[8,1,2,4096]{3,2,1,0:T(2,128)(2,1)}), bf16[8,1,2,4096]{3,2,1,0:T(2,128)(2,1)S(1)}, u32[]{:S(2)}, u32[]{:S(2)}) async-start(bf16[8,1,2,4096]{3,2,1,0:T(2,128)(2,1)} %copy.55), calls=%async_computation.3 | async-start | bytes 262144 | tf_op jit(solution)/shard_map/all_to_all | solution.py:80
  184.6 3.3 all-to-all-done.2
  188.8 67.7 %reduce-scatter.11.cloned.1.call-done = bf16[192,256]{1,0:T(8,128)(2,1)} async-done(((bf16[192,4096]{1,0:T(8,128)(2,1)}), bf16[192,256]{1,0:T(8,128)(2,1)}) %reduce-scatter.11.cloned.1.call-update) | async-done | bytes 98320 | tf_op jit(solution)/shard_map/reduce_scatter | solution.py:102
  256.6 1.6 multiply_bitcast_fusion
  258.2 74.8 %reduce-scatter.9.cloned.1.call-done = bf16[192,256]{1,0:T(8,128)(2,1)} async-done(((bf16[192,4096]{1,0:T(8,128)(2,1)}), bf16[192,256]{1,0:T(8,128)(2,1)}) %reduce-scatter.9.cloned.1.call-update) | async-done | bytes 98320 | tf_op jit(solution)/shard_map/reduce_scatter | solution.py:99
  333.0 1.6 multiply_bitcast_fusion.1
  334.5 74.4 %reduce-scatter.7.cloned.1.call-done = bf16[192,256]{1,0:T(8,128)(2,1)} async-done(((bf16[192,4096]{1,0:T(8,128)(2,1)}), bf16[192,256]{1,0:T(8,128)(2,1)}) %reduce-scatter.7.cloned.1.call-update) | async-done | bytes 98320 | tf_op jit(solution)/shard_map/reduce_scatter | solution.py:96
  408.9 1.6 multiply_bitcast_fusion.2
  (46 shorter events, 9.1 us)
Async XLA Ops:
  7.2 67.7 %copy-start = (bf16[1,192,4096]{2,1,0:T(8,128)(2,1)S(1)}, bf16[1,192,4096]{2,1,0:T(8,128)(2,1)}, u32[]{:S(2)}) copy-start(bf16[1,192,4096]{2,1,0:T(8,128)(2,1)} %param.11) | copy-start | bytes 4718596
  7.2 65.9 %all-gather.7.cloned.1.call-start = ((), (), s32[]{:S(2)}) async-start(), calls=%async_computation.12 | async-start | bytes 1179648 | tf_op jit(solution)/shard_map/all_gather | solution.py:55
  29.6 92.1 %all-gather.5.cloned.1.call-start = ((), (), s32[]{:S(2)}) async-start(), calls=%async_computation.11 | async-start | bytes 1179648 | tf_op jit(solution)/shard_map/all_gather | solution.py:56
  40.7 137.3 %reduce-scatter.5.cloned.1.call-start = ((), (), s32[]{:S(2)}) async-start(), calls=%async_computation.7 | async-start | bytes 1179648 | tf_op jit(solution)/shard_map/reduce_scatter | solution.py:74
  74.9 1.4 copy-start.2
  121.7 1.9 copy-start.4
  123.6 1.1 copy-start.1
  124.2 1.4 copy-start.3
  132.5 124.1 %reduce-scatter.11.cloned.1.call-start = ((), (), s32[]{:S(2)}) async-start(), calls=%async_computation.10 | async-start | bytes 1671168 | tf_op jit(solution)/shard_map/reduce_scatter | solution.py:102
  135.5 197.5 %reduce-scatter.9.cloned.1.call-start = ((), (), s32[]{:S(2)}) async-start(), calls=%async_computation.9 | async-start | bytes 1671168 | tf_op jit(solution)/shard_map/reduce_scatter | solution.py:99
  137.3 271.7 %reduce-scatter.7.cloned.1.call-start = ((), (), s32[]{:S(2)}) async-start(), calls=%async_computation.8 | async-start | bytes 1671168 | tf_op jit(solution)/shard_map/reduce_scatter | solution.py:96
  179.7 8.2 %all-to-all-start.2 = ((bf16[8,1,2,4096]{3,2,1,0:T(2,128)(2,1)}), bf16[8,1,2,4096]{3,2,1,0:T(2,128)(2,1)S(1)}, u32[]{:S(2)}, u32[]{:S(2)}) async-start(bf16[8,1,2,4096]{3,2,1,0:T(2,128)(2,1)} %copy.55), calls=%async_computation.3 | async-start | bytes 262144 | tf_op jit(solution)/shard_map/all_to_all | solution.py:80
Sparse Core Ops, SparseCore 0:
  29.7 43.3 all-gather.6
  76.3 45.3 all-gather.4
  132.6 45.4 reduce-scatter.4
  181.3 75.2 reduce-scatter.10
  260.2 72.7 reduce-scatter.8
  336.2 72.6 reduce-scatter.6
where the time goes:
time: 418 us; the launch traced here: 417 us
  waiting for transfers between devices  336 us (80%)
  blocking collectives  27.5 us (7%)
  local copies, waits for them, and re-layouts  15.4 us (4%)
  between operations  14.2 us (3%)
  matrix products  12.7 us (3%)
  other arithmetic  5.95 us (1%)
  starting transfers between devices  5.05 us (1%)
    reduce_scatter x1, waiting for transfers between devices, local(): lax.psum_scatter(up_term.astype(jnp.bfloat16), 'dp', scatter_dimension=1,...  74.8 us
    reduce_scatter x1, waiting for transfers between devices, local(): lax.psum_scatter(gate_term.astype(jnp.bfloat16), 'dp', scatter_dimension=...  74.4 us
    reduce_scatter x1, waiting for transfers between devices, local(): lax.psum_scatter(down_term.astype(jnp.bfloat16), 'dp', scatter_dimension=...  67.7 us
    all_gather x1, waiting for transfers between devices, local(): lax.all_gather(got_grads[:, None], 'tp', axis=1, tiled=True)  44.8 us
    reduce_scatter x1, waiting for transfers between devices, local(): lax.psum_scatter(partial_grad.reshape(n_ctx, n_tp, capacity, model_width)...  39 us
    all_gather x1, waiting for transfers between devices, local(): lax.all_gather(got_rows[:, None], 'tp', axis=1, tiled=True)  32.3 us
    all_to_all x1, blocking collectives, local(): lax.all_to_all(send_rows, 'ctx', split_axis=0, concat_axis=0, tiled=True)  19 us
    all_to_all x1, blocking collectives, local(): lax.all_to_all(send_grads, 'ctx', split_axis=0, concat_axis=0, tiled=True)  8.52 us
  transfers between devices with their start and end apart: 7, of which 7 were waited for; matrix products, arithmetic and copies ran while one was open for 4% of the time, Pallas kernels for 0%

commit v1 on v0

v1 whole, which is shorter than its diff:
```python
import functools
import math

import jax
import jax.numpy as jnp
from jax import lax
from jax.experimental import pallas as pl
from jax.experimental.pallas import tpu as pltpu
from jax.sharding import PartitionSpec as P

BF = jnp.bfloat16
F32 = jnp.float32
CHIPS = 4
CTX = 8
TOK = 4
CAP = 2
ROWS = 16


def dot(a, b):
    return jnp.dot(a, b, preferred_element_type=F32)


def dot_t(a, b):
    return lax.dot_general(a, b, (((1,), (1,)), ((), ())), preferred_element_type=F32)


def iota(shape, dim):
    return lax.broadcasted_iota(jnp.int32, shape, dim)


class Copies:
    def __init__(self, send_sems, recv_sems):
        self.send_sems, self.recv_sems = send_sems, recv_sems
        self.used = 0
        self.sent = []

    def take(self, count=1):
        self.used += count
        return self.used - count

    def make(self, src, dst, sem, device):
        return pltpu.make_async_remote_copy(
            src_ref=src,
            dst_ref=dst,
            send_sem=self.send_sems.at[sem],
            recv_sem=self.recv_sems.at[sem],
            device_id=device,
            device_id_type=pl.DeviceIdType.MESH,
        )

    def send(self, src, dst, sem, device):
        copy = self.make(src, dst, sem, device)
        copy.start()
        self.sent.append(copy)

    def arrived(self, ref, sem, device):
        self.make(ref, ref, sem, device).wait_recv()

    def drain(self):
        for copy in self.sent:
            copy.wait_send()
        self.sent = []


class PlaneGather:
    def __init__(self, copies, n_tp, ref_a, ref_b, split_b):
        self.c, self.n = copies, n_tp
        self.half = n_tp // 2
        self.a, self.b, self.split_b = ref_a, ref_b, split_b
        self.ctx, self.t = lax.axis_index("ctx"), lax.axis_index("tp")
        self.x, self.k = self.ctx // 2, self.ctx % 2
        take = copies.take
        self.sem_a1 = [take() for _ in range(CHIPS)]
        self.sem_a = {(s, d): take() for s in range(1, self.half + 1) for d in (1, -1)}
        self.sem_b = {(s, d): take() for s in range(1, self.half + 1) for d in (1, -1)}
        self.sem_x = {(o, d): take() for o in self.offsets() for d in (1, -1)}
        self.sem_f = {o: take() for o in self.offsets()}
        self.sem_sa = {o: take() for o in self.offsets()}
        self.sem_sb = {o: take() for o in self.offsets()}

    def offsets(self):
        return list(range(-(self.half - 1), self.half + 1))

    def row(self, o):
        return (self.t + o + self.n) % self.n

    def chip(self, d):
        return (self.x + d + CHIPS) % CHIPS

    def at_chip(self, d):
        return {"ctx": 2 * self.chip(d) + self.k}

    def at_row(self, d):
        return {"tp": self.row(d)}

    def sibling(self):
        return {"ctx": 2 * self.x + 1 - self.k}

    def block(self, o, d):
        return self.row(o) * CTX + self.k * CHIPS + self.chip(d)

    def four(self, o, core):
        return self.row(o) * CTX + core * CHIPS

    def pass_a(self, o, s, d):
        if s < self.half:
            ref = self.a(self.four(o, self.k), 4)
        else:
            ref = self.a(self.four(o, self.k) + (0 if d > 0 else 2), 2)
        self.c.send(ref, ref, self.sem_a[s, d], self.at_row(d))

    def wait_a(self, o, s, d):
        if s < self.half:
            ref = self.a(self.four(o, self.k), 4)
        else:
            ref = self.a(self.four(o, self.k) + (0 if d > 0 else 2), 2)
        self.c.arrived(ref, self.sem_a[s, d], self.at_row(-d))

    def part_b(self, o, s, d):
        blk = self.block(o, 0)
        return self.b(blk, 1) if s < self.half else self.split_b(blk, 0 if d > 0 else 1)

    def pass_b(self, o, s, d):
        ref = self.part_b(o, s, d)
        self.c.send(ref, ref, self.sem_b[s, d], self.at_row(d))

    def wait_b(self, o, s, d):
        self.c.arrived(self.part_b(o, s, d), self.sem_b[s, d], self.at_row(-d))

    def along_x(self, o):
        ref = self.b(self.block(o, 0), 1)
        for d in (1, -1):
            self.c.send(ref, ref, self.sem_x[o, d], self.at_chip(d))

    def turn(self, o):
        return 1 if o <= 0 else -1

    def onward_x(self, o):
        for d in (1, -1):
            self.c.arrived(self.b(self.block(o, -d), 1), self.sem_x[o, d], self.at_chip(-d))
        d = self.turn(o)
        ref = self.b(self.block(o, -d), 1)
        self.c.send(ref, ref, self.sem_f[o], self.at_chip(d))

    def to_sibling_a(self, o):
        ref = self.a(self.four(o, self.k), 4)
        self.c.send(ref, ref, self.sem_sa[o], self.sibling())

    def to_sibling_b(self, o):
        d = self.turn(o)
        self.c.arrived(self.b(self.block(o, 2), 1), self.sem_f[o], self.at_chip(-d))
        ref = self.b(self.four(o, self.k), 4)
        self.c.send(ref, ref, self.sem_sb[o], self.sibling())

    def begin(self):
        own = self.a(self.block(0, 0), 1)
        for d in range(1, CHIPS):
            self.c.send(own, own, self.sem_a1[d], self.at_chip(d))
        self.pass_b(0, 1, 1)
        self.pass_b(0, 1, -1)
        self.along_x(0)

    def rows_begin(self):
        for d in range(1, CHIPS):
            self.c.arrived(self.a(self.block(0, -d), 1), self.sem_a1[d], self.at_chip(-d))
        self.pass_a(0, 1, 1)
        self.pass_a(0, 1, -1)
        self.to_sibling_a(0)

    def at_step(self, s):
        return [-s, s] if s < self.half else [self.half]

    def step(self, s):
        last = s == self.half
        self.wait_b(self.half if last else -s, s, 1)
        self.wait_b(self.half if last else s, s, -1)
        if not last:
            self.pass_b(-s, s + 1, 1)
            self.pass_b(s, s + 1, -1)
        for o in self.at_step(s):
            self.along_x(o)
        self.wait_a(self.half if last else -s, s, 1)
        self.wait_a(self.half if last else s, s, -1)
        if not last:
            self.pass_a(-s, s + 1, 1)
            self.pass_a(s, s + 1, -1)
        for o in self.at_step(s):
            self.to_sibling_a(o)
        before = [0] if s == 1 else self.at_step(s - 1)
        for o in before:
            self.onward_x(o)
        if s > 1:
            for o in [0] if s == 2 else self.at_step(s - 2):
                self.to_sibling_b(o)

    def finish(self):
        for o in self.at_step(self.half):
            self.onward_x(o)
        if self.half > 1:
            for o in self.at_step(self.half - 1):
                self.to_sibling_b(o)
        else:
            self.to_sibling_b(0)
        for o in self.at_step(self.half):
            self.to_sibling_b(o)

    def from_sibling(self):
        for o in self.offsets():
            self.c.arrived(self.a(self.four(o, 1 - self.k), 4), self.sem_sa[o], self.sibling())
            self.c.arrived(self.b(self.four(o, 1 - self.k), 4), self.sem_sb[o], self.sibling())


def kernel(
    sizes, xd_ref, ids_ref, gates_ref, gate_hbm, up_hbm, down_hbm,
    tok_ref, gate_ref, up_ref, down_ref,
    ga, gb, g2, zp, wgu, wd, rx, rd, hb, xc, acc, part, rs_in, rs_out, xs, xr,
    send_sems, recv_sems, load_sems,
):
    n_dp, n_tp, width, units, scale = sizes
    quarter = width // 4
    half_z, half_t = n_dp // 2, n_tp // 2
    z, ctx, t = lax.axis_index("dp"), lax.axis_index("ctx"), lax.axis_index("tp")
    place = (ctx % 2) * CHIPS + ctx // 2
    me = t * CTX + place

    barrier = pltpu.get_barrier_semaphore()
    for d in range(1, n_dp):
        pl.semaphore_signal(
            barrier, inc=1, device_id={"dp": (z + d) % n_dp}, device_id_type=pl.DeviceIdType.MESH
        )
    for d in range(1, CTX):
        pl.semaphore_signal(
            barrier, inc=1, device_id={"ctx": (ctx + d) % CTX}, device_id_type=pl.DeviceIdType.MESH
        )
    rows = (1, -1) if n_tp > 2 else (1,)
    for d in rows:
        pl.semaphore_signal(
            barrier,
            inc=1,
            device_id={"tp": (t + d + n_tp) % n_tp},
            device_id_type=pl.DeviceIdType.MESH,
        )
    loads = [
        pltpu.make_async_copy(gate_hbm, wgu.at[pl.ds(0, units)], load_sems.at[0]),
        pltpu.make_async_copy(up_hbm, wgu.at[pl.ds(units, units)], load_sems.at[1]),
        pltpu.make_async_copy(down_hbm, wd, load_sems.at[2]),
    ]
    for load in loads:
        load.start()

    ga[me, :, 0:quarter] = jnp.concatenate(
        [xd_ref[:, 0:quarter], xd_ref[:, quarter : 2 * quarter]], axis=0
    ).astype(BF)
    gb[me] = jnp.concatenate(
        [xd_ref[:, 2 * quarter : 3 * quarter], xd_ref[:, 3 * quarter :]], axis=0
    ).astype(BF)
    for i in range(n_dp):
        zp[i] = jnp.concatenate(
            [xd_ref[:, 256 * i : 256 * i + 128], xd_ref[:, 256 * i + 128 : 256 * i + 256]], axis=0
        ).astype(BF)
    g2[me, z] = zp[z]
    line, lane = iota((ROWS, 128), 0), iota((ROWS, 128), 1)
    expert = line % 8
    inner = lane % ROWS
    first = ((inner // 4) * 16 + 2 * place + 1).astype(F32)
    is_grad = (inner // 4) % 2 == 1
    count = jnp.zeros((ROWS, 128), F32)
    meta = jnp.zeros((ROWS, 128), F32)
    for n in range(TOK):
        coefficient = jnp.where(expert == ids_ref[n, 0], gates_ref[n, 0], 0.0) + jnp.where(
            expert == ids_ref[n, 1], gates_ref[n, 1], 0.0
        )
        named = (expert == ids_ref[n, 0]) | (expert == ids_ref[n, 1])
        factor = jnp.where(is_grad, coefficient, 1.0)
        value = jnp.where(line < 8, first + count, factor)
        meta = jnp.where(named & (inner % 4 == n) & (lane // ROWS == place), value, meta)
        count = count + jnp.where(named, 1.0, 0.0)
    ga[me, :, quarter:] = meta.astype(BF)

    pl.semaphore_wait(barrier, n_dp - 1 + CTX - 1 + len(rows))

    copies = Copies(send_sems, recv_sems)
    plane1 = PlaneGather(
        copies,
        n_tp,
        lambda at, size: ga.at[pl.ds(at, size)],
        lambda at, size: gb.at[pl.ds(at, size)],
        lambda at, part: gb.at[pl.ds(at, 1), :, pl.ds(part * (quarter // 2), quarter // 2)],
    )
    low, quart = n_dp // 2, n_dp // 4
    plane2 = PlaneGather(
        copies,
        n_tp,
        lambda at, size: g2.at[pl.ds(at, size), pl.ds(0, low)],
        lambda at, size: g2.at[pl.ds(at, size), pl.ds(low, low)],
        lambda at, part: g2.at[pl.ds(at, 1), pl.ds(low + part * quart, quart)],
    )
    sem_z = copies.take(n_dp)
    plane1.begin()
    for d in range(1, n_dp):
        to = (z + d) % n_dp
        copies.send(zp.at[to], g2.at[me, z], sem_z + d, {"dp": to})
    plane1.rows_begin()
    for s in range(1, half_t + 1):
        plane1.step(s)
    plane1.finish()
    for d in range(1, n_dp):
        source = (z - d + n_dp) % n_dp
        copies.arrived(g2.at[me, source], sem_z + d, {"dp": source})
    plane2.begin()
    plane1.from_sibling()
    for load in loads:
        load.wait()

    table = jnp.zeros((ROWS, 128), F32)
    for r in range(n_tp):
        total = ga[r * CTX, :, quarter:].astype(F32)
        for i in range(1, CTX):
            total = total + ga[r * CTX + i, :, quarter:].astype(F32)
        slot = jnp.sum(jnp.where(line == ctx, total, 0.0), axis=0, keepdims=True)
        factor = jnp.sum(jnp.where(line == 8 + ctx, total, 0.0), axis=0, keepdims=True)
        table = table + jnp.where(line == r, slot, 0.0) + jnp.where(line == 8 + r, factor, 0.0)
    hb[z, 3 * units :, :] = table.astype(BF)

    def choosing(tab, r):
        want = tab[r : r + 1, :]
        value = tab[8 + r : 9 + r, :]
        number = (iota((64, 128), 0) + 1).astype(F32)
        return jnp.where(number == want, value, 0.0).astype(BF)

    if n_tp * CTX * CAP < 128:
        rx[...] = jnp.zeros_like(rx)
        rd[...] = jnp.zeros_like(rd)
    for r in range(n_tp):
        pick = choosing(table, r)
        for side, block in enumerate((ga, gb)):
            got = dot(pick, block[r * CTX : (r + 1) * CTX, :, 0:quarter].reshape(128, quarter))
            got = got.astype(BF)
            for h in range(2):
                at = (2 * side + h) * quarter
                rx[16 * r : 16 * r + 16, at : at + quarter] = got[32 * h : 32 * h + 16]
                rd[16 * r : 16 * r + 16, at : at + quarter] = got[32 * h + 16 : 32 * h + 32]
    both = dot_t(wgu[:, 0:quarter], rx[:, 0:quarter])
    d_hidden = dot_t(wd[:, 0:quarter], rd[:, 0:quarter])
    for j in range(1, 4):
        cols = slice(j * quarter, (j + 1) * quarter)
        both = both + dot_t(wgu[:, cols], rx[:, cols])
        d_hidden = d_hidden + dot_t(wd[:, cols], rd[:, cols])
    pre_gate, pre_up = both[:units], both[units:]
    sigmoid = 1.0 / (1.0 + jnp.exp(-pre_gate))
    activated = pre_gate * sigmoid
    d_up = d_hidden * activated
    d_gate = d_hidden * pre_up * (sigmoid * (1.0 + pre_gate * (1.0 - sigmoid)))
    hb[z, 0:units, :] = d_gate.astype(BF)
    hb[z, units : 2 * units, :] = d_up.astype(BF)
    hb[z, 2 * units : 3 * units, :] = (activated * pre_up).astype(BF)

    sem_ring = {(s, d): copies.take() for s in range(1, half_z + 1) for d in (1, -1)}
    lines = 3 * units + ROWS
    cut = (lines // 2 + 15) // 16 * 16

    def ring_part(o, s, d):
        b = (z + o + n_dp) % n_dp
        if s < half_z:
            return hb.at[b]
        return hb.at[b, pl.ds(0, cut)] if d > 0 else hb.at[b, pl.ds(cut, lines - cut)]

    def ring_send(o, s, d):
        ref = ring_part(o, s, d)
        copies.send(ref, ref, sem_ring[s, d], {"dp": (z + d + n_dp) % n_dp})

    def ring_wait(o, s, d):
        copies.arrived(ring_part(o, s, d), sem_ring[s, d], {"dp": (z - d + n_dp) % n_dp})

    ring_send(0, 1, 1)
    ring_send(0, 1, -1)

    by_slot = jnp.concatenate([d_gate, d_up], axis=0).T.astype(BF)
    step_cols = min(512, width)

    @pl.loop(0, width // step_cols)
    def _(i):
        cols = pl.ds(pl.multiple_of(i * step_cols, step_cols), step_cols)
        part[:, cols] = dot(by_slot, wgu[:, cols])

    sem_rs = {(s, d): copies.take() for s in range(1, half_t + 1) for d in (1, -1)}

    def share(o):
        u = (t + o + n_tp) % n_tp
        return part[pl.ds(pl.multiple_of(u * 16, 16), 16), :]

    def rs_slot(s, d):
        return s - 1 if d > 0 else half_t + s - 1

    def rs_send(s, d):
        total = share(half_t - s + 1 if d > 0 else s - half_t)
        if s > 1:
            total = total + rs_in[rs_slot(s - 1, d)].astype(F32)
        rs_out[rs_slot(s, d)] = total.astype(BF)
        copies.send(
            rs_out.at[rs_slot(s, d)],
            rs_in.at[rs_slot(s, d)],
            sem_rs[s, d],
            {"tp": (t + d + n_tp) % n_tp},
        )

    def rs_wait(s, d):
        copies.arrived(rs_in.at[rs_slot(s, d)], sem_rs[s, d], {"tp": (t - d + n_tp) % n_tp})

    def rs_step(s):
        if s > 1:
            rs_wait(s - 1, 1)
            if s - 1 < half_t:
                rs_wait(s - 1, -1) if s - 1 <= half_t - 1 else None
        if s <= half_t:
            rs_send(s, 1)
        if s <= half_t - 1:
            rs_send(s, -1)

    sem_ctx = copies.take(CTX)

    def to_tokens():
        total = share(0) + rs_in[rs_slot(half_t, 1)].astype(F32)
        if half_t > 1:
            total = total + rs_in[rs_slot(half_t - 1, -1)].astype(F32)
        total = total.astype(BF)
        stacked = jnp.concatenate([total[:, j * quarter : (j + 1) * quarter] for j in range(4)], 0)
        want = jnp.sum(jnp.where(line == t, table, 0.0), axis=0, keepdims=True)
        want = jnp.broadcast_to(want, (128, 128)).T[:, 0:64]
        pick = jnp.where((iota((128, 64), 1) + 1).astype(F32) == want, 1.0, 0.0).astype(BF)
        spread = dot(pick, stacked).astype(BF)
        for i in range(CTX):
            xs[i] = spread[16 * i : 16 * i + 16]
        for d in range(1, CTX):
            to = (ctx + d) % CTX
            copies.send(
                xs.at[(to % 2) * CHIPS + to // 2], xr.at[ctx], sem_ctx + d, {"ctx": to}
            )

    def tokens_out():
        total = xs[place].astype(F32)
        for d in range(1, CTX):
            source = (ctx - d + CTX) % CTX
            copies.arrived(xr.at[source], sem_ctx + d, {"ctx": source})
        for d in range(1, CTX):
            total = total + xr[(ctx - d + CTX) % CTX].astype(F32)
        for j in range(4):
            tok_ref[:, j * quarter : (j + 1) * quarter] = total[4 * j : 4 * j + 4].astype(BF)

    acc[...] = jnp.zeros_like(acc)
    if n_tp * CTX * CAP < 128:
        xc[...] = jnp.zeros_like(xc)

    def replica(o):
        b = (z + o + n_dp) % n_dp
        tab = hb[b, 3 * units :, :].astype(F32)
        for r in range(n_tp):
            got = dot(choosing(tab, r), g2[r * CTX : (r + 1) * CTX, b].reshape(128, 128))
            got = got.astype(BF)
            for h in range(2):
                for q in range(2):
                    at = (2 * h + q) * 16
                    xc[q, 16 * r : 16 * r + 16, 128 * h : 128 * h + 128] = got[at : at + 16]
        acc[0 : 2 * units, :] += dot(hb[b, 0 : 2 * units, :], xc[0])
        acc[2 * units :, :] += dot(hb[b, 2 * units : 3 * units, :], xc[1])

    def replicas(start, count, stride=1):
        lax.fori_loop(0, count, lambda i, _: (replica(start + i * stride), 0)[1], 0)

    todo = [plane2.rows_begin]
    todo += [functools.partial(plane2.step, s) for s in range(1, half_t + 1)]
    todo += [plane2.finish, plane2.from_sibling]
    grads = [functools.partial(rs_step, s) for s in range(1, half_t + 2)]
    grads += [to_tokens, tokens_out]
    done = None
    for s in range(1, half_z + 1):
        last = s == half_z
        if grads:
            grads.pop(0)()
        if todo:
            todo.pop(0)()
        ring_wait(half_z if last else -s, s, 1)
        ring_wait(half_z if last else s, s, -1)
        if not last:
            ring_send(-s, s + 1, 1)
            ring_send(s, s + 1, -1)
        if last:
            while todo:
                todo.pop(0)()
            while grads:
                grads.pop(0)()
        if not todo:
            if done is None:
                replicas(-s if not last else 1 - s, 2 * s + 1 if not last else 2 * s)
            elif not last:
                replicas(-s, 2, 2 * s)
            else:
                replicas(s, 1)
            done = s
    gate_ref[...] = acc[0:units, :] * scale
    up_ref[...] = acc[units : 2 * units, :] * scale
    down_ref[...] = acc[2 * units :, :] * scale
    copies.drain()


def sem_count(n_dp, n_tp):
    plane = CHIPS + 4 * (n_tp // 2) + 5 * n_tp
    return 2 * plane + n_dp + 2 * (n_dp // 2) + 2 * (n_tp // 2) + CTX


def local(tokens, out_grad, expert_ids, gates, gate_proj, up_proj, down_proj):
    n_dp, n_tp = lax.axis_size("dp"), lax.axis_size("tp")
    width, units = tokens.shape[1], gate_proj.shape[1]
    quarter = width // 4
    devices = n_tp * CTX
    scale = 1.0 / math.sqrt(tokens.shape[0] * n_dp * devices)
    xd = jnp.concatenate([tokens, out_grad], axis=0).astype(F32)
    vmem = pl.BlockSpec(memory_space=pltpu.VMEM)
    smem = pl.BlockSpec(memory_space=pltpu.SMEM)
    hbm = pl.BlockSpec(memory_space=pl.ANY)
    grad = jax.ShapeDtypeStruct((units, width // n_dp), F32)
    sems = sem_count(n_dp, n_tp)
    token_grad, gate_grad, up_grad, down_grad = pl.pallas_call(
        functools.partial(kernel, (n_dp, n_tp, width, units, scale)),
        out_shape=(jax.ShapeDtypeStruct(tokens.shape, BF), grad, grad, grad),
        in_specs=[vmem, smem, smem, hbm, hbm, hbm],
        out_specs=(vmem, vmem, vmem, vmem),
        scratch_shapes=[
            pltpu.VMEM((devices, ROWS, quarter + 128), BF),
            pltpu.VMEM((devices, ROWS, quarter), BF),
            pltpu.VMEM((devices, n_dp, ROWS, 128), BF),
            pltpu.VMEM((n_dp, ROWS, 128), BF),
            pltpu.VMEM((2 * units, width), BF),
            pltpu.VMEM((units, width), BF),
            pltpu.VMEM((128, width), BF),
            pltpu.VMEM((128, width), BF),
            pltpu.VMEM((n_dp, 3 * units + ROWS, 128), BF),
            pltpu.VMEM((2, 128, 256), BF),
            pltpu.VMEM((3 * units, 256), F32),
            pltpu.VMEM((128, width), F32),
            pltpu.VMEM((n_tp, 16, width), BF),
            pltpu.VMEM((n_tp, 16, width), BF),
            pltpu.VMEM((CTX, ROWS, quarter), BF),
            pltpu.VMEM((CTX, ROWS, quarter), BF),
            pltpu.SemaphoreType.DMA((sems,)),
            pltpu.SemaphoreType.DMA((sems,)),
            pltpu.SemaphoreType.DMA((3,)),
        ],
        compiler_params=pltpu.CompilerParams(
            collective_id=0, has_side_effects=True, vmem_limit_bytes=48 * 2**20
        ),
    )(
        xd,
        expert_ids,
        gates.astype(F32),
        gate_proj[0],
        up_proj[0],
        down_proj[0],
    )
    return token_grad, gate_grad[None], up_grad[None], down_grad[None]


def solution(mesh):
    rows = P(("dp", "ctx", "tp"), None)
    weights = P("ctx", "tp", None)
    grads = P("ctx", "tp", "dp")
    return jax.shard_map(
        local,
        mesh=mesh,
        in_specs=(rows, rows, rows, rows, weights, weights, weights),
        out_specs=(rows, grads, grads, grads),
        check_vma=False,
    )
```

time: 418 us -> 113 us (0.27)
  the two profiles are of different devices: /device:TPU:4 before, /device:TPU:1 now
where the time goes in v1:
time: 113 us; the launch traced here: 112 us
  Pallas kernels  102 us (90%)
  local copies, waits for them, and re-layouts  8.38 us (7%)
    pallas_call x1, Pallas kernels, local(): pl.pallas_call(functools.partial(kernel, (n_dp, n_tp, width, units, scale...  102 us
    unnamed x12, local copies, waits for them, and re-layouts  8.38 us

profile of v1, /device:TPU:1, one launch (start us, length us, event | category | flops | bytes accessed | tf_op | source)
XLA Modules:
  0.0 111.9 jit_solution(8359756269543178048)
XLA Ops:
  0.6 0.8 copy.11
  1.4 0.8 copy.12.ids_ref
  2.2 0.8 maximum_convert_fusion.xd_ref
  3.0 0.0 copy-start
  3.0 1.4 %copy-done = bf16[1,192,4096]{2,1,0:T(8,128)(2,1)S(1)} copy-done((bf16[1,192,4096]{2,1,0:T(8,128)(2,1)S(1)}, bf16[1,192,4096]{2,1,0:T(8,128)(2,1)}, u32[]{:S(2)}) %copy-start) | copy-done | bytes 1572888
  4.4 0.0 copy-start.1
  4.4 1.4 %copy-done.1 = bf16[1,192,4096]{2,1,0:T(8,128)(2,1)S(1)} copy-done((bf16[1,192,4096]{2,1,0:T(8,128)(2,1)S(1)}, bf16[1,192,4096]{2,1,0:T(8,128)(2,1)}, u32[]{:S(2)}) %copy-start.1) | copy-done | bytes 1572888
  5.8 0.0 copy-start.2
  5.8 1.4 %copy-done.2 = bf16[1,192,4096]{2,1,0:T(8,128)(2,1)S(1)} copy-done((bf16[1,192,4096]{2,1,0:T(8,128)(2,1)S(1)}, bf16[1,192,4096]{2,1,0:T(8,128)(2,1)}, u32[]{:S(2)}) %copy-start.2) | copy-done | bytes 1572888
  7.2 102.1 %shard_map.102 = (bf16[4,4096]{1,0:T(4,128)(2,1)S(1)}, f32[192,256]{1,0:T(8,128)S(1)}, f32[192,256]{1,0:T(8,128)S(1)}, f32[192,256]{1,0:T(8,128)S(1)}) custom-call(f32[8,4096]{1,0:T(8,128)S(1)} %maximum_convert_fusion.xd_ref, s32[4,2]{1,0:T(4,128)S(1)} %copy.12.ids_ref, f32[4,2]{1,0:T(4,128)S(1)} %convert_element_type.7.gates_ref, ...), custom_call_target="tpu_custom_call" | custom-call | tf_op jit(solution)/shard_map/pallas_call | solution.py:524
  109.3 0.6 copy.17
  109.9 0.7 copy.18
  110.6 0.7 copy.19
  111.2 0.7 copy.20
  (1 shorter events, 0.0 us)
Async XLA Ops:
  3.0 1.4 %copy-start = (bf16[1,192,4096]{2,1,0:T(8,128)(2,1)S(1)}, bf16[1,192,4096]{2,1,0:T(8,128)(2,1)}, u32[]{:S(2)}) copy-start(bf16[1,192,4096]{2,1,0:T(8,128)(2,1)} %param.11) | copy-start | bytes 4718596
  4.4 1.4 %copy-start.1 = (bf16[1,192,4096]{2,1,0:T(8,128)(2,1)S(1)}, bf16[1,192,4096]{2,1,0:T(8,128)(2,1)}, u32[]{:S(2)}) copy-start(bf16[1,192,4096]{2,1,0:T(8,128)(2,1)} %param.12) | copy-start | bytes 4718596
  5.8 1.4 %copy-start.2 = (bf16[1,192,4096]{2,1,0:T(8,128)(2,1)S(1)}, bf16[1,192,4096]{2,1,0:T(8,128)(2,1)}, u32[]{:S(2)}) copy-start(bf16[1,192,4096]{2,1,0:T(8,128)(2,1)} %param.13) | copy-start | bytes 4718596

commit v2 on v1

v2 whole, which is shorter than its diff:
```python
import functools
import math

import jax
import jax.numpy as jnp
from jax import lax
from jax.experimental import pallas as pl
from jax.experimental.pallas import tpu as pltpu
from jax.sharding import PartitionSpec as P

BF = jnp.bfloat16
F32 = jnp.float32
CHIPS = 4
CTX = 8
TOK = 4
CAP = 2
PIECES = 4
RS_AT = 2
SPLIT = 2
ROWS = 16


def dot(a, b):
    return jnp.dot(a, b, preferred_element_type=F32)


def dot_t(a, b):
    return lax.dot_general(a, b, (((1,), (1,)), ((), ())), preferred_element_type=F32)


def iota(shape, dim):
    return lax.broadcasted_iota(jnp.int32, shape, dim)


class Copies:
    def __init__(self, send_sems, recv_sems):
        self.send_sems, self.recv_sems = send_sems, recv_sems
        self.used = 0
        self.sent = []

    def take(self, count=1):
        self.used += count
        return self.used - count

    def make(self, src, dst, sem, device):
        return pltpu.make_async_remote_copy(
            src_ref=src,
            dst_ref=dst,
            send_sem=self.send_sems.at[sem],
            recv_sem=self.recv_sems.at[sem],
            device_id=device,
            device_id_type=pl.DeviceIdType.MESH,
        )

    def send(self, src, dst, sem, device):
        copy = self.make(src, dst, sem, device)
        copy.start()
        self.sent.append(copy)

    def arrived(self, ref, sem, device):
        self.make(ref, ref, sem, device).wait_recv()

    def drain(self):
        for copy in self.sent:
            copy.wait_send()
        self.sent = []


class Plane:
    def __init__(self, copies, n_tp):
        self.c, self.n, self.half = copies, n_tp, n_tp // 2
        ctx, self.t = lax.axis_index("ctx"), lax.axis_index("tp")
        self.x, self.k = ctx // 2, ctx % 2
        self.sibling = {"ctx": 2 * self.x + 1 - self.k}

    def offsets(self):
        return list(range(-(self.half - 1), self.half + 1))

    def row(self, o):
        return (self.t + o + self.n) % self.n

    def chip(self, d):
        return (self.x + d + CHIPS) % CHIPS

    def at_chip(self, d):
        return {"ctx": 2 * self.chip(d) + self.k}

    def at_row(self, d):
        return {"tp": self.row(d)}

    def block(self, o, d):
        return self.row(o) * CTX + self.k * CHIPS + self.chip(d)

    def four(self, o, core):
        return self.row(o) * CTX + core * CHIPS

    def at_step(self, s):
        return [0] if s == 0 else [-s, s] if s < self.half else [self.half]


class ChipsFirst(Plane):
    def __init__(self, copies, n_tp, ref):
        super().__init__(copies, n_tp)
        self.ref = ref
        self.sem_x = [copies.take() for _ in range(CHIPS)]
        self.sem_y = {
            (s, d, e): copies.take()
            for s in range(1, self.half + 1)
            for d in (1, -1)
            for e in range(CHIPS)
            if self.goes(s, d, e)
        }
        self.sem_s = {o: copies.take() for o in self.offsets()}

    def goes(self, s, d, e):
        return s < self.half or (e < 2) == (d > 0)

    def send(self, o, s, d, e):
        if self.goes(s, d, e):
            ref = self.ref(self.block(o, -e), 1)
            self.c.send(ref, ref, self.sem_y[s, d, e], self.at_row(d))

    def wait(self, o, s, d, e):
        if self.goes(s, d, e):
            ref = self.ref(self.block(o, -e), 1)
            self.c.arrived(ref, self.sem_y[s, d, e], self.at_row(-d))

    def begin(self):
        own = self.ref(self.block(0, 0), 1)
        for d in (1, 3, 2):
            self.c.send(own, own, self.sem_x[d], self.at_chip(d))
        self.send(0, 1, 1, 0)
        self.send(0, 1, -1, 0)

    def rows_begin(self):
        for e in (1, 3, 2):
            self.c.arrived(self.ref(self.block(0, -e), 1), self.sem_x[e], self.at_chip(-e))
            self.send(0, 1, 1, e)
            self.send(0, 1, -1, e)
        self.to_sibling(0)

    def step(self, s):
        last = s == self.half
        for e in (0, 1, 3, 2):
            self.wait(self.half if last else -s, s, 1, e)
            if not last:
                self.send(-s, s + 1, 1, e)
            self.wait(self.half if last else s, s, -1, e)
            if not last:
                self.send(s, s + 1, -1, e)
        for o in self.at_step(s):
            self.to_sibling(o)

    def to_sibling(self, o):
        ref = self.ref(self.four(o, self.k), 4)
        self.c.send(ref, ref, self.sem_s[o], self.sibling)

    def from_sibling(self, o):
        self.c.arrived(self.ref(self.four(o, 1 - self.k), 4), self.sem_s[o], self.sibling)


class RowsFirst(Plane):
    def __init__(self, copies, n_tp, ref, split):
        super().__init__(copies, n_tp)
        self.ref, self.split = ref, split
        steps = range(1, self.half + 1)
        self.sem_y = {(s, d): copies.take() for s in steps for d in (1, -1)}
        self.sem_x = {(o, d): copies.take() for o in self.offsets() for d in (1, -1)}
        self.sem_f = {o: copies.take() for o in self.offsets()}
        self.sem_s = {o: copies.take() for o in self.offsets()}

    def part(self, o, s, d):
        at = self.block(o, 0)
        return self.ref(at, 1) if s < self.half else self.split(at, 0 if d > 0 else 1)

    def send(self, o, s, d):
        ref = self.part(o, s, d)
        self.c.send(ref, ref, self.sem_y[s, d], self.at_row(d))

    def wait(self, o, s, d):
        self.c.arrived(self.part(o, s, d), self.sem_y[s, d], self.at_row(-d))

    def begin(self):
        self.send(0, 1, 1)
        self.send(0, 1, -1)

    def step(self, s):
        last = s == self.half
        self.wait(self.half if last else -s, s, 1)
        if not last:
            self.send(-s, s + 1, 1)
        self.wait(self.half if last else s, s, -1)
        if not last:
            self.send(s, s + 1, -1)

    def along(self, s):
        for o in self.at_step(s):
            ref = self.ref(self.block(o, 0), 1)
            for d in (1, -1):
                self.c.send(ref, ref, self.sem_x[o, d], self.at_chip(d))

    def turn(self, o):
        return 1 if o <= 0 else -1

    def onward(self, s):
        for o in self.at_step(s):
            for d in (1, -1):
                self.c.arrived(self.ref(self.block(o, -d), 1), self.sem_x[o, d], self.at_chip(-d))
            d = self.turn(o)
            ref = self.ref(self.block(o, -d), 1)
            self.c.send(ref, ref, self.sem_f[o], self.at_chip(d))

    def to_sibling(self, s):
        for o in self.at_step(s):
            d = self.turn(o)
            self.c.arrived(self.ref(self.block(o, 2), 1), self.sem_f[o], self.at_chip(-d))
            ref = self.ref(self.four(o, self.k), 4)
            self.c.send(ref, ref, self.sem_s[o], self.sibling)

    def from_sibling(self, o):
        self.c.arrived(self.ref(self.four(o, 1 - self.k), 4), self.sem_s[o], self.sibling)


def kernel(
    sizes, xd_ref, gate_hbm, up_hbm, down_hbm,
    tok_ref, gate_ref, up_ref, down_ref,
    ga, gb, g2, zp, wgu, wd, rx, rd, hb, xc, acc, part, rs_in, rs_out, xs, xr,
    send_sems, recv_sems, load_sems,
):
    n_dp, n_tp, width, units, scale = sizes
    quarter = width // 4
    half_z, half_t = n_dp // 2, n_tp // 2
    z, ctx, t = lax.axis_index("dp"), lax.axis_index("ctx"), lax.axis_index("tp")
    place = (ctx % 2) * CHIPS + ctx // 2
    me = t * CTX + place

    barrier = pltpu.get_barrier_semaphore()
    for d in range(1, n_dp):
        pl.semaphore_signal(
            barrier, inc=1, device_id={"dp": (z + d) % n_dp}, device_id_type=pl.DeviceIdType.MESH
        )
    for d in range(1, CTX):
        pl.semaphore_signal(
            barrier, inc=1, device_id={"ctx": (ctx + d) % CTX}, device_id_type=pl.DeviceIdType.MESH
        )
    rows = (1, -1) if n_tp > 2 else (1,)
    for d in rows:
        pl.semaphore_signal(
            barrier,
            inc=1,
            device_id={"tp": (t + d + n_tp) % n_tp},
            device_id_type=pl.DeviceIdType.MESH,
        )
    loads = [
        pltpu.make_async_copy(gate_hbm, wgu.at[pl.ds(0, units)], load_sems.at[0]),
        pltpu.make_async_copy(up_hbm, wgu.at[pl.ds(units, units)], load_sems.at[1]),
        pltpu.make_async_copy(down_hbm, wd, load_sems.at[2]),
    ]
    for load in loads:
        load.start()

    def stacked_rows(first, size):
        halves = [xd_ref[0:8, at : at + size] for at in (first, first + size)]
        return jnp.concatenate(halves, axis=0).astype(BF)

    ga[me, :, 0:quarter] = stacked_rows(0, quarter)
    gb[me] = stacked_rows(2 * quarter, quarter)
    for i in range(n_dp):
        zp[i] = stacked_rows(256 * i, 128)
    g2[me, z] = zp[z]
    line, lane = iota((ROWS, 128), 0), iota((ROWS, 128), 1)
    expert = (line % 8).astype(F32)
    inner = lane % ROWS
    first = ((inner // 4) * 16 + 2 * place + 1).astype(F32)
    is_grad = (inner // 4) % 2 == 1
    count = jnp.zeros((ROWS, 128), F32)
    meta = jnp.zeros((ROWS, 128), F32)
    routing = xd_ref[8:16, 0:128]
    for n in range(TOK):
        named, coefficient = line < 0, jnp.zeros((ROWS, 128), F32)
        for k in range(2):
            chosen = expert == routing[k : k + 1, n : n + 1]
            named = named | chosen
            coefficient = jnp.where(chosen, routing[k + 2 : k + 3, n : n + 1], coefficient)
        factor = jnp.where(is_grad, coefficient, 1.0)
        value = jnp.where(line < 8, first + count, factor)
        meta = jnp.where(named & (inner % 4 == n) & (lane // ROWS == place), value, meta)
        count = count + jnp.where(named, 1.0, 0.0)
    ga[me, :, quarter:] = meta.astype(BF)

    pl.semaphore_wait(barrier, n_dp - 1 + CTX - 1 + len(rows))

    copies = Copies(send_sems, recv_sems)
    a1 = ChipsFirst(copies, n_tp, lambda at, size: ga.at[pl.ds(at, size)])
    b1 = RowsFirst(
        copies,
        n_tp,
        lambda at, size: gb.at[pl.ds(at, size)],
        lambda at, part: gb.at[pl.ds(at, 1), :, pl.ds(part * (quarter // 2), quarter // 2)],
    )
    low = n_dp // 2
    a2 = ChipsFirst(copies, n_tp, lambda at, size: g2.at[pl.ds(at, size), pl.ds(0, low)])
    b2 = RowsFirst(
        copies,
        n_tp,
        lambda at, size: g2.at[pl.ds(at, size), pl.ds(low, low)],
        lambda at, part: g2.at[pl.ds(at, 1), pl.ds(low + part * (low // 2), low // 2)],
    )
    sem_z = copies.take(n_dp)

    def columns_send():
        for d in range(1, n_dp):
            to = (z + d) % n_dp
            copies.send(zp.at[to], g2.at[me, z], sem_z + d, {"dp": to})

    def columns_begin():
        for d in range(1, n_dp):
            source = (z - d + n_dp) % n_dp
            copies.arrived(g2.at[me, source], sem_z + d, {"dp": source})
        b2.begin()
        b2.along(0)
        a2.begin()

    begin_at = min(2, half_t)
    b1.begin()
    a1.begin()
    b1.along(0)
    columns_send()
    b1.step(1)
    b1.along(1)
    a1.rows_begin()
    b2_steps = 0
    for s in range(1, half_t + 1):
        if s < half_t:
            b1.step(s + 1)
            b1.along(s + 1)
        b1.onward(s - 1)
        if s == half_t:
            b1.onward(s)
        if s > 1:
            b1.to_sibling(s - 2)
        if s == begin_at:
            columns_begin()
        elif s > begin_at:
            b2_steps += 1
            b2.step(b2_steps)
            b2.along(b2_steps)
        a1.step(s)
    b1.to_sibling(half_t - 1)
    b1.to_sibling(half_t)
    if b2_steps + 1 < half_t:
        b2_steps += 1
        b2.step(b2_steps)
        b2.along(b2_steps)
    a2.rows_begin()
    for o in a1.offsets():
        a1.from_sibling(o)
        b1.from_sibling(o)
    for load in loads:
        load.wait()

    table = jnp.zeros((ROWS, 128), F32)
    for r in range(n_tp):
        total = ga[r * CTX, :, quarter:].astype(F32)
        for i in range(1, CTX):
            total = total + ga[r * CTX + i, :, quarter:].astype(F32)
        slot = jnp.sum(jnp.where(line == ctx, total, 0.0), axis=0, keepdims=True)
        factor = jnp.sum(jnp.where(line == 8 + ctx, total, 0.0), axis=0, keepdims=True)
        table = table + jnp.where(line == r, slot, 0.0) + jnp.where(line == 8 + r, factor, 0.0)
    hb[z, 3 * units :, :] = table.astype(BF)

    def choosing(tab, r):
        want = tab[r : r + 1, :]
        value = tab[8 + r : 9 + r, :]
        number = (iota((64, 128), 0) + 1).astype(F32)
        return jnp.where(number == want, value, 0.0).astype(BF)

    if n_tp * CTX * CAP < 128:
        rx[...] = jnp.zeros_like(rx)
        rd[...] = jnp.zeros_like(rd)
    for r in range(n_tp):
        pick = choosing(table, r)
        for side, block in enumerate((ga, gb)):
            got = dot(pick, block[r * CTX : (r + 1) * CTX, :, 0:quarter].reshape(128, quarter))
            got = got.astype(BF)
            for h in range(2):
                at = (2 * side + h) * quarter
                rx[16 * r : 16 * r + 16, at : at + quarter] = got[32 * h : 32 * h + 16]
                rd[16 * r : 16 * r + 16, at : at + quarter] = got[32 * h + 16 : 32 * h + 32]
    both = dot_t(wgu[:, 0:quarter], rx[:, 0:quarter])
    d_hidden = dot_t(wd[:, 0:quarter], rd[:, 0:quarter])
    for j in range(1, 4):
        cols = slice(j * quarter, (j + 1) * quarter)
        both = both + dot_t(wgu[:, cols], rx[:, cols])
        d_hidden = d_hidden + dot_t(wd[:, cols], rd[:, cols])
    pre_gate, pre_up = both[:units], both[units:]
    sigmoid = 1.0 / (1.0 + jnp.exp(-pre_gate))
    activated = pre_gate * sigmoid
    d_up = d_hidden * activated
    d_gate = d_hidden * pre_up * (sigmoid * (1.0 + pre_gate * (1.0 - sigmoid)))
    hb[z, 0:units, :] = d_gate.astype(BF)
    hb[z, units : 2 * units, :] = d_up.astype(BF)
    hb[z, 2 * units : 3 * units, :] = (activated * pre_up).astype(BF)

    lines = 3 * units + ROWS
    cuts = [lines * c // (16 * PIECES) * 16 for c in range(PIECES + 1)]
    pieces = range(PIECES)

    def ring_goes(s, d, c):
        return s < half_z or (c < PIECES // 2) == (d > 0)

    sem_ring = {
        (s, d, c): copies.take()
        for s in range(1, half_z + 1)
        for d in (1, -1)
        for c in pieces
        if ring_goes(s, d, c)
    }

    def ring_part(o, c):
        return hb.at[(z + o + n_dp) % n_dp, pl.ds(cuts[c], cuts[c + 1] - cuts[c])]

    def ring_send(o, s, d, c):
        if ring_goes(s, d, c):
            ref = ring_part(o, c)
            copies.send(ref, ref, sem_ring[s, d, c], {"dp": (z + d + n_dp) % n_dp})

    def ring_wait(o, s, d, c):
        if ring_goes(s, d, c):
            copies.arrived(ring_part(o, c), sem_ring[s, d, c], {"dp": (z - d + n_dp) % n_dp})

    for c in pieces:
        ring_send(0, 1, 1, c)
        ring_send(0, 1, -1, c)

    by_slot = jnp.concatenate([d_gate, d_up], axis=0).T.astype(BF)
    step_cols = min(512, width)

    @pl.loop(0, width // step_cols)
    def _(i):
        cols = pl.ds(pl.multiple_of(i * step_cols, step_cols), step_cols)
        part[:, cols] = dot(by_slot, wgu[:, cols])

    wide = width // SPLIT
    sem_rs = {
        (s, d, c): copies.take() for s in range(1, half_t + 1) for d in (1, -1) for c in range(SPLIT)
    }

    def share(o, c):
        at = pl.multiple_of((t + o + n_tp) % n_tp * 16, 16)
        return part[pl.ds(at, 16), c * wide : (c + 1) * wide]

    def rs_slot(s, d, c):
        return (s - 1 if d > 0 else half_t + s - 1) * SPLIT + c

    def rs_wait(s, d, c):
        ref = rs_in.at[rs_slot(s, d, c)]
        copies.arrived(ref, sem_rs[s, d, c], {"tp": (t - d + n_tp) % n_tp})

    def rs_send(s, d, c):
        total = share(half_t - s + 1 if d > 0 else s - half_t, c)
        if s > 1:
            rs_wait(s - 1, d, c)
            total = total + rs_in[rs_slot(s - 1, d, c)].astype(F32)
        slot = rs_slot(s, d, c)
        rs_out[slot] = total.astype(BF)
        copies.send(
            rs_out.at[slot], rs_in.at[slot], sem_rs[s, d, c], {"tp": (t + d + n_tp) % n_tp}
        )

    def rs_step(s):
        for c in range(SPLIT):
            rs_send(s, 1, c)
            if s < half_t:
                rs_send(s, -1, c)

    sem_ctx = copies.take(CTX)

    def to_tokens():
        totals = []
        for c in range(SPLIT):
            rs_wait(half_t, 1, c)
            total = share(0, c) + rs_in[rs_slot(half_t, 1, c)].astype(F32)
            if half_t > 1:
                rs_wait(half_t - 1, -1, c)
                total = total + rs_in[rs_slot(half_t - 1, -1, c)].astype(F32)
            total = total.astype(BF)
            totals += [total[:, j * quarter : (j + 1) * quarter] for j in range(wide // quarter)]
        stacked = jnp.concatenate(totals, axis=0)
        want = jnp.sum(jnp.where(line == t, table, 0.0), axis=0, keepdims=True)
        want = jnp.broadcast_to(want, (128, 128)).T[:, 0:64]
        pick = jnp.where((iota((128, 64), 1) + 1).astype(F32) == want, 1.0, 0.0).astype(BF)
        spread = dot(pick, stacked).astype(BF)
        for i in range(CTX):
            xs[i] = spread[16 * i : 16 * i + 16]
        for d in range(1, CTX):
            to = (ctx + d) % CTX
            copies.send(
                xs.at[(to % 2) * CHIPS + to // 2], xr.at[ctx], sem_ctx + d, {"ctx": to}
            )

    def tokens_out():
        total = xs[place].astype(F32)
        for d in range(1, CTX):
            source = (ctx - d + CTX) % CTX
            copies.arrived(xr.at[source], sem_ctx + d, {"ctx": source})
        for d in range(1, CTX):
            total = total + xr[(ctx - d + CTX) % CTX].astype(F32)
        for j in range(4):
            tok_ref[:, j * quarter : (j + 1) * quarter] = total[4 * j : 4 * j + 4].astype(BF)

    acc[...] = jnp.zeros_like(acc)
    if n_tp * CTX * CAP < 128:
        xc[...] = jnp.zeros_like(xc)

    def replicas(*offsets):
        numbers = [(z + o + n_dp) % n_dp for o in offsets]
        for i, b in enumerate(numbers):
            tab = hb[b, 3 * units :, :].astype(F32)
            for r in range(n_tp):
                got = dot(choosing(tab, r), g2[r * CTX : (r + 1) * CTX, b].reshape(128, 128))
                got = got.astype(BF)
                row = 128 * i + 16 * r
                for h in range(2):
                    for q in range(2):
                        at = (2 * h + q) * 16
                        xc[q, row : row + 16, 128 * h : 128 * h + 128] = got[at : at + 16]
        used = 128 * len(numbers)
        for q, first, count in ((0, 0, 2 * units), (1, 2 * units, units)):
            rows = [hb[b, first : first + count, :] for b in numbers]
            acc[first : first + count, :] += dot(jnp.concatenate(rows, axis=1), xc[q, 0:used])

    def all_from_sibling():
        for o in b2.offsets():
            a2.from_sibling(o)
            b2.from_sibling(o)

    plan = {s: [] for s in range(1, half_z + 1)}

    def at(s, *tasks):
        plan[min(s, half_z)] += tasks

    for s in range(b2_steps + 1, half_t + 1):
        at(s - b2_steps, functools.partial(b2.step, s), functools.partial(b2.along, s))
    for s in range(1, half_t + 1):
        at(s, functools.partial(a2.step, s))
        at(s + RS_AT, functools.partial(rs_step, s))
    for s in range(half_t + 1):
        at(max(s, 1) + 1, functools.partial(b2.onward, s))
        at(max(s, 1) + 2, functools.partial(b2.to_sibling, s))
    at(half_t + 2, all_from_sibling)
    at(half_t + 1 + RS_AT, to_tokens)
    at(half_t + 3 + RS_AT, tokens_out)
    ready = min(half_t + 2, half_z)
    waiting = [(0,)]
    for s in range(1, half_z + 1):
        last = s == half_z
        for task in plan[s]:
            task()
        for c in pieces:
            for d in (1, -1):
                ring_wait(half_z if last else -d * s, s, d, c)
                if not last:
                    ring_send(-d * s, s + 1, d, c)
            if s >= ready and waiting:
                replicas(*waiting.pop(0))
        waiting.append((-s, s) if not last else (half_z,))
    for offsets in waiting:
        replicas(*offsets)
    gate_ref[...] = acc[0:units, :] * scale
    up_ref[...] = acc[units : 2 * units, :] * scale
    down_ref[...] = acc[2 * units :, :] * scale
    copies.drain()


def sem_count(n_dp, n_tp):
    rows = 2 * (n_tp // 2)
    chips_first = 2 * (CHIPS + CHIPS * rows + n_tp)
    rows_first = rows + 4 * n_tp
    return chips_first + 2 * rows_first + n_dp + n_dp * PIECES + rows * SPLIT + CTX


def local(tokens, out_grad, expert_ids, gates, gate_proj, up_proj, down_proj):
    n_dp, n_tp = lax.axis_size("dp"), lax.axis_size("tp")
    width, units = tokens.shape[1], gate_proj.shape[1]
    quarter = width // 4
    devices = n_tp * CTX
    scale = 1.0 / math.sqrt(tokens.shape[0] * n_dp * devices)
    routing = jnp.concatenate([expert_ids.T.astype(F32), gates.T.astype(F32)], axis=0)
    routing = jnp.pad(routing, ((0, 4), (0, width - TOK)))
    xd = jnp.concatenate([tokens.astype(F32), out_grad.astype(F32), routing], axis=0)
    vmem = pl.BlockSpec(memory_space=pltpu.VMEM)
    hbm = pl.BlockSpec(memory_space=pl.ANY)
    grad = jax.ShapeDtypeStruct((units, width // n_dp), F32)
    sems = sem_count(n_dp, n_tp)
    token_grad, gate_grad, up_grad, down_grad = pl.pallas_call(
        functools.partial(kernel, (n_dp, n_tp, width, units, scale)),
        out_shape=(jax.ShapeDtypeStruct(tokens.shape, BF), grad, grad, grad),
        in_specs=[vmem, hbm, hbm, hbm],
        out_specs=(vmem, vmem, vmem, vmem),
        scratch_shapes=[
            pltpu.VMEM((devices, ROWS, quarter + 128), BF),
            pltpu.VMEM((devices, ROWS, quarter), BF),
            pltpu.VMEM((devices, n_dp, ROWS, 128), BF),
            pltpu.VMEM((n_dp, ROWS, 128), BF),
            pltpu.VMEM((2 * units, width), BF),
            pltpu.VMEM((units, width), BF),
            pltpu.VMEM((128, width), BF),
            pltpu.VMEM((128, width), BF),
            pltpu.VMEM((n_dp, 3 * units + ROWS, 128), BF),
            pltpu.VMEM((2, 256, 256), BF),
            pltpu.VMEM((3 * units, 256), F32),
            pltpu.VMEM((128, width), F32),
            pltpu.VMEM((n_tp * SPLIT, 16, width // SPLIT), BF),
            pltpu.VMEM((n_tp * SPLIT, 16, width // SPLIT), BF),
            pltpu.VMEM((CTX, ROWS, quarter), BF),
            pltpu.VMEM((CTX, ROWS, quarter), BF),
            pltpu.SemaphoreType.DMA((sems,)),
            pltpu.SemaphoreType.DMA((sems,)),
            pltpu.SemaphoreType.DMA((3,)),
        ],
        compiler_params=pltpu.CompilerParams(
            collective_id=0, has_side_effects=True, vmem_limit_bytes=52 * 2**20
        ),
    )(
        xd,
        gate_proj[0],
        up_proj[0],
        down_proj[0],
    )
    return token_grad, gate_grad[None], up_grad[None], down_grad[None]


def solution(mesh):
    rows = P(("dp", "ctx", "tp"), None)
    weights = P("ctx", "tp", None)
    grads = P("ctx", "tp", "dp")
    return jax.shard_map(
        local,
        mesh=mesh,
        in_specs=(rows, rows, rows, rows, weights, weights, weights),
        out_specs=(rows, grads, grads, grads),
        check_vma=False,
    )
```

time: 113 us -> 92.5 us (0.82)
  Pallas kernels: 102 us -> 86 us
  local copies, waits for them, and re-layouts: 8.38 us -> 2.65 us
  other arithmetic: 0.81 us -> 2.93 us
    pallas_call x1, Pallas kernels: 102 us -> 86 us  [local(): pl.pallas_call(functools.partial(kernel, (n_dp, n_tp, width, units, scale...]
    unnamed x12 -> x4, local copies, waits for them, and re-layouts: 8.38 us -> 2.65 us
    convert_element_type x2 -> x4, other arithmetic: 0.81 us -> 2.88 us  [the longest x1 0.77 us: local(): out_grad.astype(F32)]
where the time goes in v2:
time: 92.5 us; the launch traced here: 92.2 us
  Pallas kernels  86 us (93%)
  other arithmetic  2.93 us (3%)
  local copies, waits for them, and re-layouts  2.65 us (3%)
    pallas_call x1, Pallas kernels, local(): pl.pallas_call(functools.partial(kernel, (n_dp, n_tp, width, units, scale...  86 us
    unnamed x4, local copies, waits for them, and re-layouts  2.65 us

profile of v2, /device:TPU:1, one launch (start us, length us, event | category | flops | bytes accessed | tf_op | source)
XLA Modules:
  0.0 92.2 jit_solution(4952061057006472981)
XLA Ops:
  0.6 0.7 convert_bitcast_fusion.1
  1.3 0.7 convert_bitcast_fusion
  2.0 0.8 convert_element_type.20
  2.7 0.8 convert_element_type.21
  3.6 86.0 %shard_map.102 = (bf16[4,4096]{1,0:T(4,128)(2,1)S(1)}, f32[192,256]{1,0:T(8,128)S(1)}, f32[192,256]{1,0:T(8,128)S(1)}, f32[192,256]{1,0:T(8,128)S(1)}) custom-call(f32[16,4096]{1,0:T(8,128)S(1)} %pad_maximum_fusion.xd_ref, bf16[192,4096]{1,0:T(8,128)(2,1)} %bitcast.13, bf16[192,4096]{1,0:T(8,128)(2,1)} %bitcast.14, bf16[192,4096]{1,0:T(8,128)(2,1)} %bitcast.15), custom_call_target="tpu_custom_call" | custom-call | tf_op jit(solution)/shard_map/pallas_call | solution.py:596
  89.6 0.6 copy.15
  90.2 0.7 copy.16
  90.9 0.7 copy.17
  91.6 0.7 copy.18
  (2 shorter events, 0.1 us)

commit v3 on v2

--- a/solution.py
+++ b/solution.py
@@ -15,6 +15,7 @@
 TOK = 4
 CAP = 2
 PIECES = 4
+DRAIN = 32
 RS_AT = 2
 SPLIT = 2
 ROWS = 16
@@ -60,10 +61,11 @@
     def arrived(self, ref, sem, device):
         self.make(ref, ref, sem, device).wait_recv()
 
-    def drain(self):
-        for copy in self.sent:
+    def drain(self, count=None):
+        count = len(self.sent) if count is None else count
+        for copy in self.sent[:count]:
             copy.wait_send()
-        self.sent = []
+        self.sent = self.sent[count:]
 
 
 class Plane:
@@ -99,9 +101,9 @@
 
 
 class ChipsFirst(Plane):
-    def __init__(self, copies, n_tp, ref):
+    def __init__(self, copies, n_tp, ref, grouped=False):
         super().__init__(copies, n_tp)
-        self.ref = ref
+        self.ref, self.grouped = ref, grouped
         self.sem_x = [copies.take() for _ in range(CHIPS)]
         self.sem_y = {
             (s, d, e): copies.take()
@@ -113,30 +115,44 @@
         self.sem_s = {o: copies.take() for o in self.offsets()}
 
     def goes(self, s, d, e):
+        if self.grouped:
+            return e == 0
         return s < self.half or (e < 2) == (d > 0)
+
+    def piece(self, o, s, d, e):
+        if not self.grouped:
+            return self.ref(self.block(o, -e), 1)
+        if s < self.half:
+            return self.ref(self.four(o, self.k), 4)
+        return self.ref(self.four(o, self.k) + (0 if d > 0 else 2), 2)
 
     def send(self, o, s, d, e):
         if self.goes(s, d, e):
-            ref = self.ref(self.block(o, -e), 1)
+            ref = self.piece(o, s, d, e)
             self.c.send(ref, ref, self.sem_y[s, d, e], self.at_row(d))
 
     def wait(self, o, s, d, e):
         if self.goes(s, d, e):
-            ref = self.ref(self.block(o, -e), 1)
+            ref = self.piece(o, s, d, e)
             self.c.arrived(ref, self.sem_y[s, d, e], self.at_row(-d))
 
     def begin(self):
         own = self.ref(self.block(0, 0), 1)
         for d in (1, 3, 2):
             self.c.send(own, own, self.sem_x[d], self.at_chip(d))
-        self.send(0, 1, 1, 0)
-        self.send(0, 1, -1, 0)
+        if not self.grouped:
+            self.send(0, 1, 1, 0)
+            self.send(0, 1, -1, 0)
 
     def rows_begin(self):
         for e in (1, 3, 2):
             self.c.arrived(self.ref(self.block(0, -e), 1), self.sem_x[e], self.at_chip(-e))
-            self.send(0, 1, 1, e)
-            self.send(0, 1, -1, e)
+            if not self.grouped:
+                self.send(0, 1, 1, e)
+                self.send(0, 1, -1, e)
+        if self.grouped:
+            self.send(0, 1, 1, 0)
+            self.send(0, 1, -1, 0)
         self.to_sibling(0)
 
     def step(self, s):
@@ -222,7 +238,7 @@
 
 
 def kernel(
-    sizes, xd_ref, gate_hbm, up_hbm, down_hbm,
+    sizes, xd_ref, routing_ref, gate_hbm, up_hbm, down_hbm,
     tok_ref, gate_ref, up_ref, down_ref,
     ga, gb, g2, zp, wgu, wd, rx, rd, hb, xc, acc, part, rs_in, rs_out, xs, xr,
     send_sems, recv_sems, load_sems,
@@ -275,7 +291,7 @@
     is_grad = (inner // 4) % 2 == 1
     count = jnp.zeros((ROWS, 128), F32)
     meta = jnp.zeros((ROWS, 128), F32)
-    routing = xd_ref[8:16, 0:128]
+    routing = routing_ref[...]
     for n in range(TOK):
         named, coefficient = line < 0, jnp.zeros((ROWS, 128), F32)
         for k in range(2):
@@ -299,7 +315,7 @@
         lambda at, part: gb.at[pl.ds(at, 1), :, pl.ds(part * (quarter // 2), quarter // 2)],
     )
     low = n_dp // 2
-    a2 = ChipsFirst(copies, n_tp, lambda at, size: g2.at[pl.ds(at, size), pl.ds(0, low)])
+    a2 = ChipsFirst(copies, n_tp, lambda at, size: g2.at[pl.ds(at, size), pl.ds(0, low)], grouped=True)
     b2 = RowsFirst(
         copies,
         n_tp,
@@ -540,14 +556,14 @@
     def at(s, *tasks):
         plan[min(s, half_z)] += tasks
 
+    for s in range(half_t + 1):
+        at(max(s, 1), functools.partial(b2.onward, s))
+        at(max(s, 1) + 1, functools.partial(b2.to_sibling, s))
     for s in range(b2_steps + 1, half_t + 1):
         at(s - b2_steps, functools.partial(b2.step, s), functools.partial(b2.along, s))
     for s in range(1, half_t + 1):
         at(s, functools.partial(a2.step, s))
         at(s + RS_AT, functools.partial(rs_step, s))
-    for s in range(half_t + 1):
-        at(max(s, 1) + 1, functools.partial(b2.onward, s))
-        at(max(s, 1) + 2, functools.partial(b2.to_sibling, s))
     at(half_t + 2, all_from_sibling)
     at(half_t + 1 + RS_AT, to_tokens)
     at(half_t + 3 + RS_AT, tokens_out)
@@ -564,6 +580,8 @@
                     ring_send(-d * s, s + 1, d, c)
             if s >= ready and waiting:
                 replicas(*waiting.pop(0))
+        if 1 < s < half_z:
+            copies.drain(DRAIN)
         waiting.append((-s, s) if not last else (half_z,))
     for offsets in waiting:
         replicas(*offsets)
@@ -586,9 +604,8 @@
     quarter = width // 4
     devices = n_tp * CTX
     scale = 1.0 / math.sqrt(tokens.shape[0] * n_dp * devices)
-    routing = jnp.concatenate([expert_ids.T.astype(F32), gates.T.astype(F32)], axis=0)
-    routing = jnp.pad(routing, ((0, 4), (0, width - TOK)))
-    xd = jnp.concatenate([tokens.astype(F32), out_grad.astype(F32), routing], axis=0)
+    xd = jnp.concatenate([tokens, out_grad], axis=0).astype(F32)
+    routing = jnp.concatenate([expert_ids.T.astype(BF), gates.T], axis=0).astype(F32)
     vmem = pl.BlockSpec(memory_space=pltpu.VMEM)
     hbm = pl.BlockSpec(memory_space=pl.ANY)
     grad = jax.ShapeDtypeStruct((units, width // n_dp), F32)
@@ -596,7 +613,7 @@
     token_grad, gate_grad, up_grad, down_grad = pl.pallas_call(
         functools.partial(kernel, (n_dp, n_tp, width, units, scale)),
         out_shape=(jax.ShapeDtypeStruct(tokens.shape, BF), grad, grad, grad),
-        in_specs=[vmem, hbm, hbm, hbm],
+        in_specs=[vmem, vmem, hbm, hbm, hbm],
         out_specs=(vmem, vmem, vmem, vmem),
         scratch_shapes=[
             pltpu.VMEM((devices, ROWS, quarter + 128), BF),
@@ -624,6 +641,7 @@
         ),
     )(
         xd,
+        routing,
         gate_proj[0],
         up_proj[0],
         down_proj[0],

time: 92.5 us -> 91.4 us (0.988)
    convert_element_type x4 -> x3, other arithmetic: 2.88 us -> 2.15 us  [the longest x1 0.81 us: local(): xd = jnp.concatenate([tokens, out_grad], axis=0).astype(F32)]
where the time goes in v3:
time: 91.4 us; the launch traced here: 91.2 us
  Pallas kernels  85.7 us (94%)
  local copies, waits for them, and re-layouts  2.65 us (3%)
  other arithmetic  2.15 us (2%)
    pallas_call x1, Pallas kernels, local(): pl.pallas_call(functools.partial(kernel, (n_dp, n_tp, width, units, scale...  85.7 us
    unnamed x4, local copies, waits for them, and re-layouts  2.65 us

profile of v3, /device:TPU:1, one launch (start us, length us, event | category | flops | bytes accessed | tf_op | source)
XLA Modules:
  0.0 91.2 jit_solution(15415072642509300921)
XLA Ops:
  0.6 0.7 convert_bitcast_fusion
  1.3 0.7 maximum_convert_fusion.1.routing_ref
  2.0 0.8 maximum_convert_fusion.xd_ref
  2.8 85.7 %shard_map.102 = (bf16[4,4096]{1,0:T(4,128)(2,1)S(1)}, f32[192,256]{1,0:T(8,128)S(1)}, f32[192,256]{1,0:T(8,128)S(1)}, f32[192,256]{1,0:T(8,128)S(1)}) custom-call(f32[8,4096]{1,0:T(8,128)S(1)} %maximum_convert_fusion.xd_ref, f32[4,4]{1,0:T(4,128)S(1)} %maximum_convert_fusion.1.routing_ref, bf16[192,4096]{1,0:T(8,128)(2,1)} %bitcast.12, ...), custom_call_target="tpu_custom_call" | custom-call | tf_op jit(solution)/shard_map/pallas_call | solution.py:613
  88.5 0.6 copy.15
  89.1 0.7 copy.16
  89.8 0.7 copy.17
  90.5 0.7 copy.18
